TPU v7x, 32 devices: a whole 2x2x4 slice. The times are simulated.
32 devices in a mesh: row: 4 (over y, core), col: 8 (over z, x).
Axes of the slice: x: 2, y: 2, z: 4, core: 2. Of those that a mesh axis runs over, the one named last changes fastest.
Arguments:
- trailing_inverse: float32 [6144, 6144], P('row', 'col'), may hold values from -6 to 6
- factor_cols: float32 [3, 6144, 256], P(None, ('col', 'row')), may hold values from -0.078125 to 0.078125
- factor_blocks: float32 [3, 256, 256], replicated, may hold values from -0.375 to 0.375
- diag_inverse: float32 [3, 256, 256], replicated, may hold values from -6 to 6
Outputs:
- inv_cols: float32 [3, 6144, 256], P(None, ('row', 'col'))
- inv_diag: float32 [3, 256, 256], replicated
- inv_cross: float32 [3, 256, 256], replicated
All inputs are finite; a program needn't handle non-finite values.
Results may differ from a plain program's by a relative error of at most 0.0001.
Values sent between devices are 32-bit elements; how exact they have to be, the bound alone decides.
A program may use at most 128 MiB of HBM per device.

v0:
```python
import jax
import jax.numpy as jnp
from jax import lax
from jax.sharding import PartitionSpec as P


def product(left, right):
    return jnp.dot(left, right, precision=lax.Precision.HIGHEST, preferred_element_type=jnp.float32)


def pair_order(node_count):
    return [
        (later_node, target_node)
        for target_node in reversed(range(node_count))
        for later_node in range(target_node + 1, node_count)
    ]


def per_device(trailing_inverse, factor_cols, factor_blocks, diag_inverse):
    node_count = factor_cols.shape[0]
    piece_rows = factor_cols.shape[1]
    node_width = factor_cols.shape[2]
    row_count = lax.axis_size("row")
    col_count = lax.axis_size("col")
    row_index = lax.axis_index("row")
    col_index = lax.axis_index("col")
    col_ratio = col_count // row_count
    sub_rows = piece_rows // row_count
    pair_list = pair_order(node_count)
    node_groups = [[node_index] for node_index in reversed(range(node_count))]
    own_cols = [None] * node_count
    own_factor = [None] * node_count
    blocks = {}
    for node_group in node_groups:
        first_node = min(node_group)
        group_size = len(node_group)
        gathered = lax.all_gather(
            factor_cols[first_node : first_node + group_size], "row", axis=1, tiled=True
        )
        partial_value = jnp.einsum(
            "rc,mcw->rmw",
            trailing_inverse,
            gathered,
            precision=lax.Precision.HIGHEST,
            preferred_element_type=jnp.float32,
        )
        partial_value = partial_value.reshape(trailing_inverse.shape[0], group_size * node_width)
        sender = gathered.reshape(group_size, row_count, row_count, sub_rows, node_width)
        sender = lax.dynamic_index_in_dim(sender, row_index, 2, keepdims=False)
        sender = jnp.broadcast_to(
            sender[:, None], (group_size, col_ratio, row_count, sub_rows, node_width)
        )
        sender = sender.reshape(group_size, col_count * sub_rows, node_width)
        received = lax.all_to_all(
            lax.all_to_all(sender, "col", split_axis=1, concat_axis=1, tiled=True),
            "row",
            split_axis=1,
            concat_axis=1,
            tiled=True,
        )
        received = received.reshape(group_size, row_count, col_ratio, sub_rows, node_width)
        own_rows = lax.dynamic_index_in_dim(received, col_index // row_count, 2, keepdims=False)
        own_rows = own_rows.reshape(group_size, piece_rows, node_width)
        reduced = lax.psum_scatter(partial_value, "col", scatter_dimension=0, tiled=True)
        for target_node in node_group:
            slot = target_node - first_node
            value = reduced
            for later_node in range(target_node + 1, node_count):
                value = value + product(
                    own_cols[later_node], factor_blocks[pair_list.index((later_node, target_node))]
                )
            own_cols[target_node] = -value
            own_factor[target_node] = own_rows[slot]
        term_list = []
        for target_node in node_group:
            for later_node in range(target_node + 1, node_count):
                term_list.append(product(own_cols[later_node].T, own_factor[target_node]))
            term_list.append(product(own_factor[target_node].T, own_cols[target_node]))
        block_totals = lax.psum(jnp.stack(term_list), ("row", "col"))
        cursor = 0
        for target_node in node_group:
            for later_node in range(target_node + 1, node_count):
                value_sum = block_totals[cursor]
                cursor = cursor + 1
                for other_node in range(target_node + 1, node_count):
                    if later_node >= other_node:
                        block_value = blocks[later_node, other_node]
                    else:
                        block_value = blocks[other_node, later_node].T
                    value_sum = value_sum + product(
                        block_value, factor_blocks[pair_list.index((other_node, target_node))]
                    )
                blocks[later_node, target_node] = -value_sum
            diag_term = block_totals[cursor]
            cursor = cursor + 1
            for later_node in range(target_node + 1, node_count):
                diag_term = diag_term + product(
                    factor_blocks[pair_list.index((later_node, target_node))].T,
                    blocks[later_node, target_node],
                )
            blocks[target_node, target_node] = diag_inverse[target_node] - diag_term
    inv_cols = jnp.stack(own_cols)
    inv_diag = jnp.stack([blocks[node_index, node_index] for node_index in range(node_count)])
    inv_cross = jnp.stack([blocks[slot_pair] for slot_pair in pair_list])
    return (inv_cols, inv_diag, inv_cross)


def solution(mesh):
    return jax.shard_map(
        per_device,
        mesh=mesh,
        in_specs=(P("row", "col"), P(None, ("col", "row"), None), P(), P()),
        out_specs=(P(None, ("row", "col"), None), P(), P()),
        check_vma=False,
    )
```

profile of v0, /device:TPU:0, one launch (start us, length us, event | category | flops | bytes accessed | tf_op | source)
XLA Modules:
  0.0 388.7 jit_solution(1548812748816781921)
XLA Ops:
  7.2 1.2 fusion.46
  8.4 10.1 %all_gather.10 = f32[1,768,256]{2,1,0:T(8,128)S(1)} all-gather(f32[1,192,256]{2,1,0:T(8,128)S(1)} %get-tuple-element.8), channel_id=1, replica_groups=mesh['row'=4,'col'=8] {'row'}, dimensions={1}, use_global_device_ids=true | all-gather | bytes 983040 | tf_op jit(solution)/shard_map/all_gather | solution.py:37
  18.4 7.4 %fusion.13 = f32[1536,256]{1,0:T(8,128)} fusion(f32[1536,768]{1,0:T(8,128)} %param.4, f32[1,768,256]{2,1,0:T(8,128)S(1)} %all_gather.10), kind=kOutput, calls=%fused_computation.33 | convolution fusion | flops 3623878656 | bytes 7077888 | tf_op jit(solution)/shard_map/rc,mcw->rmw/dot_general | solution.py:40
  25.9 8.7 %all_gather.11 = f32[1,768,256]{2,1,0:T(8,128)S(1)} all-gather(f32[1,192,256]{2,1,0:T(8,128)S(1)} %get-tuple-element.7), channel_id=1, replica_groups=mesh['row'=4,'col'=8] {'row'}, dimensions={1}, use_global_device_ids=true | all-gather | bytes 983040 | tf_op jit(solution)/shard_map/all_gather | solution.py:37
  34.6 7.4 %fusion.11 = f32[1536,256]{1,0:T(8,128)} fusion(f32[1536,768]{1,0:T(8,128)} %param.4, f32[1,768,256]{2,1,0:T(8,128)S(1)} %all_gather.11), kind=kOutput, calls=%fused_computation.31 | convolution fusion | flops 3623878656 | bytes 7077888 | tf_op jit(solution)/shard_map/rc,mcw->rmw/dot_general | solution.py:40
  42.0 8.7 %all_gather.9 = f32[1,768,256]{2,1,0:T(8,128)S(1)} all-gather(f32[1,192,256]{2,1,0:T(8,128)S(1)} %get-tuple-element.6), channel_id=1, replica_groups=mesh['row'=4,'col'=8] {'row'}, dimensions={1}, use_global_device_ids=true | all-gather | bytes 983040 | tf_op jit(solution)/shard_map/all_gather | solution.py:37
  50.8 1.1 broadcast_in_dim.32
  51.9 5.8 %all-to-all-start = ((f32[1,384,256]{2,0,1:T(1,128)}), f32[1,384,256]{2,0,1:T(1,128)S(1)}, u32[]{:S(2)}, u32[]{:S(2)}) async-start(f32[1,384,256]{2,0,1:T(1,128)} %broadcast_in_dim.32), calls=%async_computation.3 | async-start | bytes 786432 | tf_op jit(solution)/shard_map/all_to_all | solution.py:55
  58.0 7.4 %fusion.15 = f32[1536,256]{1,0:T(8,128)} fusion(f32[1536,768]{1,0:T(8,128)} %param.4, f32[1,768,256]{2,1,0:T(8,128)S(1)} %all_gather.9), kind=kOutput, calls=%fused_computation.35 | convolution fusion | flops 3623878656 | bytes 7077888 | tf_op jit(solution)/shard_map/rc,mcw->rmw/dot_general | solution.py:40
  65.5 1.1 broadcast_in_dim.38
  66.6 3.3 all-to-all-done
  69.9 3.6 all-to-all-start.4
  74.0 14.9 %all-to-all-done.4 = f32[1,384,256]{2,0,1:T(1,128)S(1)} async-done(((f32[1,384,256]{2,0,1:T(1,128)}), f32[1,384,256]{2,0,1:T(1,128)S(1)}, u32[]{:S(2)}, u32[]{:S(2)}) %all-to-all-start.4) | async-done | bytes 393248 | tf_op jit(solution)/shard_map/all_to_all | solution.py:55
  88.9 14.5 %all_to_all.30 = f32[1,384,256]{2,0,1:T(1,128)} all-to-all(f32[1,384,256]{2,0,1:T(1,128)S(1)} %broadcast_in_dim.35), channel_id=1, replica_groups=mesh['row'=4,'col'=8] {'col'}, dimensions={1} | all-to-all | bytes 786432 | tf_op jit(solution)/shard_map/all_to_all | solution.py:55
  103.4 9.8 %all_to_all.31 = f32[1,384,256]{2,0,1:T(1,128)S(1)} all-to-all(f32[1,384,256]{2,0,1:T(1,128)S(1)} %all-to-all-done), channel_id=1, replica_groups=mesh['row'=4,'col'=8] {'row'}, dimensions={1} | all-to-all | bytes 786432 | tf_op jit(solution)/shard_map/all_to_all | solution.py:54
  113.2 9.8 %all_to_all.32 = f32[1,384,256]{2,0,1:T(1,128)S(1)} all-to-all(f32[1,384,256]{2,0,1:T(1,128)S(1)} %all-to-all-done.4), channel_id=1, replica_groups=mesh['row'=4,'col'=8] {'row'}, dimensions={1} | all-to-all | bytes 786432 | tf_op jit(solution)/shard_map/all_to_all | solution.py:54
  123.0 3.5 all-to-all-start.3
  127.0 6.9 %all-to-all-done.3 = f32[1,384,256]{2,0,1:T(1,128)S(1)} async-done(((f32[1,384,256]{2,0,1:T(1,128)}), f32[1,384,256]{2,0,1:T(1,128)S(1)}, u32[]{:S(2)}, u32[]{:S(2)}) %all-to-all-start.3) | async-done | bytes 393248 | tf_op jit(solution)/shard_map/all_to_all | solution.py:54
  134.3 28.4 %reduce-scatter.8.cloned.1.call-done = f32[192,256]{1,0:T(8,128)} async-done(((f32[1536,256]{1,0:T(8,128)}), f32[192,256]{1,0:T(8,128)}) %reduce-scatter.8.cloned.1.call-update) | async-done | bytes 196624 | tf_op jit(solution)/shard_map/reduce_scatter | solution.py:64
  162.6 1.4 fusion.10
  165.4 64.4 %reduce-scatter.4.cloned.1.call-done = f32[192,256]{1,0:T(8,128)} async-done(((f32[1536,256]{1,0:T(8,128)}), f32[192,256]{1,0:T(8,128)}) %reduce-scatter.4.cloned.1.call-update) | async-done | bytes 196624 | tf_op jit(solution)/shard_map/reduce_scatter | solution.py:64
  229.8 1.3 convolution_add_fusion.6
  231.1 1.3 fusion.9
  233.1 1.6 convolution_bitcast_fusion.5
  237.1 1.4 convolution_bitcast_fusion.3
  239.4 131.2 %all-reduce.3.cloned.1.call-done = (f32[1,256,256]{2,1,0:T(8,128)}, f32[2,256,256]{2,1,0:T(8,128)}, f32[3,256,256]{2,1,0:T(8,128)}) async-done(((f32[1,256,256]{2,1,0:T(8,128)}, f32[2,256,256]{2,1,0:T(8,128)}, f32[3,256,256]{2,1,0:T(8,128)}), (f32[1,256,256]{2,1,0:T(8,128)}, f32[2,256,256]{2,1,0:T(8,128)}, f32[3,256,256]{2,1,0:T(8,128)})) %all-reduce.3.cloned.1.call-update) | async-done | bytes 1572880 | tf_op jit(solution)/shard_map/psum | solution.py:79
  370.6 1.0 slice_subtract_fusion
  371.6 1.3 fusion.8
  372.9 1.6 fusion.7
  374.5 1.3 convolution_add_fusion.1
  375.8 1.3 convolution_add_fusion.3
  377.8 1.6 fusion.4
  (40 shorter events, 10.4 us)
Async XLA Ops:
  7.2 127.1 %reduce-scatter.6.cloned.1.call-start = ((), (), s32[]{:S(2)}) async-start(), calls=%async_computation.10 | async-start | bytes 1769472 | tf_op jit(solution)/shard_map/reduce_scatter | solution.py:64
  25.8 136.8 %reduce-scatter.8.cloned.1.call-start = ((), (), s32[]{:S(2)}) async-start(), calls=%async_computation.11 | async-start | bytes 1769472 | tf_op jit(solution)/shard_map/reduce_scatter | solution.py:64
  51.9 18.0 %all-to-all-start = ((f32[1,384,256]{2,0,1:T(1,128)}), f32[1,384,256]{2,0,1:T(1,128)S(1)}, u32[]{:S(2)}, u32[]{:S(2)}) async-start(f32[1,384,256]{2,0,1:T(1,128)} %broadcast_in_dim.32), calls=%async_computation.3 | async-start | bytes 786432 | tf_op jit(solution)/shard_map/all_to_all | solution.py:55
  57.7 172.1 %reduce-scatter.4.cloned.1.call-start = ((), (), s32[]{:S(2)}) async-start(), calls=%async_computation.9 | async-start | bytes 1769472 | tf_op jit(solution)/shard_map/reduce_scatter | solution.py:64
  65.4 97.2 %copy-start = (f32[3,256,256]{2,1,0:T(8,128)S(1)}, f32[3,256,256]{2,1,0:T(8,128)}, u32[]{:S(2)}) copy-start(f32[3,256,256]{2,1,0:T(8,128)} %param.6) | copy-start | bytes 2359300
  69.9 19.0 %all-to-all-start.4 = ((f32[1,384,256]{2,0,1:T(1,128)}), f32[1,384,256]{2,0,1:T(1,128)S(1)}, u32[]{:S(2)}, u32[]{:S(2)}) async-start(f32[1,384,256]{2,0,1:T(1,128)} %broadcast_in_dim.38), calls=%async_computation.7 | async-start | bytes 786432 | tf_op jit(solution)/shard_map/all_to_all | solution.py:55
  123.0 10.9 %all-to-all-start.3 = ((f32[1,384,256]{2,0,1:T(1,128)}), f32[1,384,256]{2,0,1:T(1,128)S(1)}, u32[]{:S(2)}, u32[]{:S(2)}) async-start(f32[1,384,256]{2,0,1:T(1,128)} %all_to_all.30), calls=%async_computation.6 | async-start | bytes 786432 | tf_op jit(solution)/shard_map/all_to_all | solution.py:54
  126.5 244.1 %all-reduce.3.cloned.1.call-start = ((), (), s32[]{:S(2)}) async-start(), calls=%async_computation.12 | async-start | bytes 3145728 | tf_op jit(solution)/shard_map/psum | solution.py:79
  162.6 72.9 %copy-start.1 = (f32[192,256]{1,0:T(8,128)S(1)}, f32[192,256]{1,0:T(8,128)}, u32[]{:S(2)}) copy-start(f32[192,256]{1,0:T(8,128)} %reduce-scatter.8.cloned.1.call-done) | copy-start | bytes 589828
  231.1 139.5 %copy-start.2 = (f32[3,256,256]{2,1,0:T(8,128)S(1)}, f32[3,256,256]{2,1,0:T(8,128)}, u32[]{:S(2)}) copy-start(f32[3,256,256]{2,1,0:T(8,128)} %param.7) | copy-start | bytes 2359300
Sparse Core Ops, SparseCore 0:
  26.0 69.1 reduce-scatter.5
  98.9 63.6 reduce-scatter.7
  166.1 63.7 reduce-scatter.3
  238.7 131.8 all-reduce.2
where the time goes:
time: 390 us; the launch traced here: 389 us
  waiting for transfers between devices  249 us (64%)
  blocking collectives  61.6 us (16%)
  matrix products  40.4 us (10%)
  between operations  14.1 us (4%)
  starting transfers between devices  13.5 us (3%)
  other arithmetic  5.48 us (1%)
  local copies, waits for them, and re-layouts  4.45 us (1%)
    psum x1, waiting for transfers between devices, per_device(): block_totals = lax.psum(jnp.stack(term_list), ('row', 'col'))  131 us
    reduce_scatter x3, waiting for transfers between devices, per_device(): lax.psum_scatter(partial_value, 'col', scatter_dimension=0, tiled=True)  92.8 us
    all_gather x3, blocking collectives, per_device(): lax.all_gather(factor_cols[first_node:first_node + group_size], 'row', ax...  27.5 us
    dot_general x3, matrix products, per_device(): jnp.einsum('rc,mcw->rmw', trailing_inverse, gathered, precision=lax.Preci...  22.1 us
    all_to_all x2, blocking collectives, per_device(): lax.all_to_all(lax.all_to_all(sender, 'col', split_axis=1, concat_axis=1,...  19.6 us
    dot_general x17, matrix products, product(): jnp.dot(left, right, precision=lax.Precision.HIGHEST, preferred_element_t...  18.3 us
    all_to_all x2, waiting for transfers between devices, per_device(): lax.all_to_all(sender, 'col', split_axis=1, concat_axis=1, tiled=True)  18.2 us
    all_to_all x1, blocking collectives, per_device(): lax.all_to_all(sender, 'col', split_axis=1, concat_axis=1, tiled=True)  14.5 us
  transfers between devices with their start and end apart: 7, of which 6 were waited for; matrix products, arithmetic and copies ran while one was open for 6% of the time, Pallas kernels for 0%

commit v1 on v0

v1 whole, which is shorter than its diff:
```python
import functools

import jax
import jax.numpy as jnp
from jax import lax
from jax.experimental import pallas as pl
from jax.experimental.pallas import tpu as pltpu
from jax.sharding import PartitionSpec as P

MESH = pl.DeviceIdType.MESH
CORES = 2


def exact_dot(left, right, left_dim=1):
    return lax.dot_general(
        left,
        right,
        (((left_dim,), (0,)), ((), ())),
        precision=lax.Precision.HIGHEST,
        preferred_element_type=jnp.float32,
    )


def split(value):
    high = value.astype(jnp.bfloat16)
    low = (value - high.astype(jnp.float32)).astype(jnp.bfloat16)
    return high, low


def pair_order(node_count):
    return [
        (later_node, target_node)
        for target_node in reversed(range(node_count))
        for later_node in range(target_node + 1, node_count)
    ]


def row_splits(rows, row_count, col_count):
    splits = row_count
    while splits > 1 and rows % (splits * col_count * 8):
        splits //= 2
    return splits


def kernel(
    sizes,
    t_hbm,
    f_ref,
    b_ref,
    d_ref,
    v_ref,
    diag_ref,
    cross_ref,
    t_ref,
    fg,
    fh,
    fl,
    g,
    xr,
    zr,
    fown,
    *rest,
):
    row_count, col_count, nx, ny, nz, nodes, piece, width = sizes
    stages = [rest[0:4], rest[4:8]]
    send_sem, recv_sem, t_sem = rest[8:]
    r = lax.axis_index("row")
    c = lax.axis_index("col")
    y, core = r // CORES, r % CORES
    z, x = c // nx, c % nx
    total = row_count * col_count
    me = r * col_count + c
    pairs = pair_order(nodes)

    t_copy = pltpu.make_async_copy(t_hbm, t_ref, t_sem)
    t_copy.start()

    barrier = pltpu.get_barrier_semaphore()

    def greet(step, carry):
        other = (me + step) % total
        pl.semaphore_signal(
            barrier, inc=1, device_id=(other // col_count, other % col_count), device_id_type=MESH
        )
        return carry

    lax.fori_loop(1, total, greet, 0)
    pl.semaphore_wait(barrier, total - 1)

    def remote(src, dst, sem, row, col):
        return pltpu.make_async_remote_copy(
            src_ref=src,
            dst_ref=dst,
            send_sem=send_sem.at[sem],
            recv_sem=recv_sem.at[sem],
            device_id=(row, col),
            device_id_type=MESH,
        )

    order = list(reversed(range(nodes)))
    base = 0
    started = []
    sibling = y * CORES + 1 - core

    def rows_of(row):
        return pl.ds(pl.multiple_of(row * piece, 8), piece)

    across, inside, relayed = {}, {}, {}
    for node in order:
        for dy in range(1, ny):
            target = ((y + dy) % ny) * CORES + core
            across[node, dy] = remote(f_ref.at[node], fg.at[node, rows_of(r)], base, target, c)
            base += 1
            source = ((y - dy + ny) % ny) * CORES + core
            landed = fg.at[node, rows_of(source)]
            relayed[node, dy] = remote(landed, landed, base, sibling, c)
            base += 1
        inside[node] = remote(f_ref.at[node], fg.at[node, rows_of(r)], base, sibling, c)
        base += 1
    for node in order:
        for dy in range(1, ny):
            across[node, dy].start()
        inside[node].start()

    place = c * row_count + r
    own_row, own_col = place // col_count, place % col_count
    stays = place == me
    owned = remote(f_ref, fown, base, own_row, own_col)
    base += 1

    @pl.when(jnp.logical_not(stays))
    def _():
        owned.start()

    @pl.when(stays)
    def _():
        fown[...] = f_ref[...]

    x_base = base
    base += nodes * nz * (nx - 1)

    def x_copy(node, dz, dx):
        target = (x + dx) % nx
        return remote(
            g.at[node, dz, rows_of(target)],
            xr.at[node, dz, dx - 1],
            x_base + (node * nz + dz) * (nx - 1) + dx - 1,
            r,
            z * nx + target,
        )

    for node in order:
        fg[node, rows_of(r)] = f_ref[node]
    t_copy.wait()
    for node in order:
        for dy in range(1, ny):
            across[node, dy].wait_recv()
            relayed[node, dy].start()
        inside[node].wait_recv()
        for dy in range(1, ny):
            relayed[node, dy].wait_recv()
        high, low = split(fg[node])
        fh[...] = high
        fl[...] = low

        def produce(dz, carry):
            target = (z + dz + 1) % nz
            start = target * (nx * piece)
            span = min(nx, CORES) * piece
            for at in range(0, nx * piece, span):
                rows = pl.ds(pl.multiple_of(start + at, 8), span)
                t_high, t_low = split(t_ref[rows])
                value = jnp.dot(t_high, fh[...], preferred_element_type=jnp.float32)
                value += jnp.dot(t_low, fh[...], preferred_element_type=jnp.float32)
                value += jnp.dot(t_high, fl[...], preferred_element_type=jnp.float32)
                g[node, dz, at : at + span] = value
            for dx in range(1, nx):
                x_copy(node, dz, dx).start()
            return carry

        lax.fori_loop(0, nz, produce, 0)

    z_base = base
    base += nodes * (nz - 1)

    def z_copy(node, dz):
        target = (z + dz + 1) % nz
        return remote(
            g.at[node, dz, rows_of(x)],
            zr.at[node, dz],
            z_base + node * (nz - 1) + dz,
            r,
            target * nx + x,
        )

    def forward(node, dz):
        value = g[node, dz, rows_of(x)]
        for dx in range(1, nx):
            x_copy(node, dz, dx).wait_recv()
            value += xr[node, dz, dx - 1]
        g[node, dz, rows_of(x)] = value
        if dz < nz - 1:
            z_copy(node, dz).start()

    def finish(node):
        value = g[node, nz - 1, rows_of(x)]
        for dz in range(nz - 1):
            z_copy(node, dz).wait_recv()
            value += zr[node, dz]
        for later in range(node + 1, nodes):
            value += exact_dot(v_ref[later], b_ref[pairs.index((later, node))])
        v_ref[node] = -value

    class Total:
        def __init__(self, refs, sem):
            self.part, self.first, self.second, self.out = refs
            rows = self.part.shape[0]
            self.splits = row_splits(rows, row_count, col_count)
            self.share = rows // self.splits
            self.small = self.share // col_count
            self.sem = sem
            self.copies = []

        def share_of(self, row):
            return pl.ds(pl.multiple_of((row % self.splits) * self.share, 8), self.share)

        def small_of(self, col):
            start = (r % self.splits) * self.share + col * self.small
            return pl.ds(pl.multiple_of(start, 8), self.small)

        def send(self, src, dst, row, col):
            copy = remote(src, dst, self.sem, row, col)
            self.sem += 1
            copy.start()
            started.append(copy)
            self.copies.append(copy)

        def receive(self):
            for copy in self.copies:
                copy.wait_recv()
            self.copies = []

        def step1(self):
            for dr in range(1, row_count):
                row = (r + dr) % row_count
                self.send(self.part.at[self.share_of(row)], self.first.at[r], row, c)
            self.first[r] = self.part[self.share_of(r)]

        def step2(self):
            self.receive()
            value = self.first[0]
            for row in range(1, row_count):
                value += self.first[row]
            self.part[self.share_of(r)] = value
            for dc in range(1, col_count):
                col = (c + dc) % col_count
                self.send(self.part.at[self.small_of(col)], self.second.at[c], r, col)
            self.second[c] = self.part[self.small_of(c)]

        def step3(self):
            self.receive()
            value = self.second[0]
            for col in range(1, col_count):
                value += self.second[col]
            self.out[self.small_of(c)] = value
            for dc in range(1, col_count):
                ref = self.out.at[self.small_of(c)]
                self.send(ref, ref, r, (c + dc) % col_count)

        def step4(self):
            self.receive()
            group = (r // self.splits) * self.splits
            for dr in range(1, self.splits):
                ref = self.out.at[self.share_of(r)]
                self.send(ref, ref, group + (r - group + dr) % self.splits, c)

    per_total = 2 * (row_count - 1) + 2 * (col_count - 1)
    many, last = Total(stages[0], base), Total(stages[1], base + per_total)

    def block(ref, index):
        return ref.at[index * width : (index + 1) * width]

    slots = {}
    early = []
    for node in order[:-1]:
        slots[node, node] = len(early)
        early.append((node, node))
        for target in reversed(range(node)):
            slots[node, target] = len(early)
            early.append((node, target))

    for node in order[:-1]:
        for dz in range(nz):
            forward(node, dz)

    @pl.when(jnp.logical_not(stays))
    def _():
        owned.wait()

    def contribute(node):
        block(many.part, slots[node, node])[...] = exact_dot(fown[node], v_ref[node], 0)
        for target in reversed(range(node)):
            block(many.part, slots[node, target])[...] = exact_dot(v_ref[node], fown[target], 0)

    for node in order[:-2]:
        finish(node)
        contribute(node)
    for dz in range(nz - 1):
        forward(0, dz)
    if nodes > 1:
        finish(1)
        contribute(1)
        many.step1()
    forward(0, nz - 1)
    many.step2()
    finish(0)
    last.part[...] = exact_dot(fown[0], v_ref[0], 0)
    last.step1()
    many.step3()
    last.step2()
    many.step4()
    last.step3()
    many.receive()

    for node in order:
        for later in range(node + 1, nodes):
            value = block(many.out, slots[later, node])[...]
            for other in range(node + 1, nodes):
                factor = b_ref[pairs.index((other, node))]
                if later == other:
                    value += exact_dot(diag_ref[other], factor)
                elif later > other:
                    value += exact_dot(cross_ref[pairs.index((later, other))], factor)
                else:
                    value += exact_dot(cross_ref[pairs.index((other, later))], factor, 0)
            cross_ref[pairs.index((later, node))] = -value
        value = d_ref[node]
        if node > 0:
            value -= block(many.out, slots[node, node])[...]
        for later in range(node + 1, nodes):
            pair = pairs.index((later, node))
            value -= exact_dot(b_ref[pair], cross_ref[pair], 0)
        diag_ref[node] = value
    last.step4()
    last.receive()
    diag_ref[0] = diag_ref[0] - last.out[...]

    for copy in started:
        copy.wait_send()
    for node in order:
        for dy in range(1, ny):
            across[node, dy].wait_send()
            relayed[node, dy].wait_send()
        inside[node].wait_send()
        for dz in range(nz):
            for dx in range(1, nx):
                x_copy(node, dz, dx).wait_send()
            if dz < nz - 1:
                z_copy(node, dz).wait_send()


def per_device(trailing_inverse, factor_cols, factor_blocks, diag_inverse):
    nodes, piece, width = factor_cols.shape
    row_count = lax.axis_size("row")
    col_count = lax.axis_size("col")
    ny = row_count // CORES
    nx = ny if col_count % ny == 0 else 1
    nz = col_count // nx
    depth = trailing_inverse.shape[1]
    sizes = (row_count, col_count, nx, ny, nz, nodes, piece, width)
    pair_count = factor_blocks.shape[0]

    def f32(*shape):
        return pltpu.VMEM(shape, jnp.float32)

    def total_refs(blocks):
        rows = blocks * width
        share = rows // row_splits(rows, row_count, col_count)
        return [
            f32(rows, width),
            f32(row_count, share, width),
            f32(col_count, share // col_count, width),
            f32(rows, width),
        ]

    early = pair_count + nodes - 1
    copies = (
        nodes * (2 * (ny - 1) + 1)
        + 1
        + nodes * nz * (nx - 1)
        + nodes * (nz - 1)
        + 4 * (row_count - 1 + col_count - 1)
    )
    vmem = pl.BlockSpec(memory_space=pltpu.VMEM)
    return pl.pallas_call(
        functools.partial(kernel, sizes),
        out_shape=(
            jax.ShapeDtypeStruct((nodes, piece, width), jnp.float32),
            jax.ShapeDtypeStruct((nodes, width, width), jnp.float32),
            jax.ShapeDtypeStruct((pair_count, width, width), jnp.float32),
        ),
        in_specs=[pl.BlockSpec(memory_space=pl.ANY), vmem, vmem, vmem],
        out_specs=(vmem, vmem, vmem),
        scratch_shapes=[
            f32(*trailing_inverse.shape),
            f32(nodes, depth, width),
            pltpu.VMEM((depth, width), jnp.bfloat16),
            pltpu.VMEM((depth, width), jnp.bfloat16),
            f32(nodes, nz, nx * piece, width),
            f32(nodes, nz, max(nx - 1, 1), piece, width),
            f32(nodes, max(nz - 1, 1), piece, width),
            f32(nodes, piece, width),
            *total_refs(early),
            *total_refs(1),
            pltpu.SemaphoreType.DMA((copies,)),
            pltpu.SemaphoreType.DMA((copies,)),
            pltpu.SemaphoreType.DMA,
        ],
        compiler_params=pltpu.CompilerParams(
            collective_id=0, has_side_effects=True, vmem_limit_bytes=61 * 1024 * 1024
        ),
    )(trailing_inverse, factor_cols, factor_blocks, diag_inverse)


def solution(mesh):
    return jax.shard_map(
        per_device,
        mesh=mesh,
        in_specs=(P("row", "col"), P(None, ("col", "row"), None), P(), P()),
        out_specs=(P(None, ("row", "col"), None), P(), P()),
        check_vma=False,
    )
```

time: 390 us -> 137 us (0.35)
  waiting for transfers between devices: 249 us -> 0 us
  Pallas kernels: 0 us -> 129 us
  blocking collectives: 61.6 us -> 0 us
  matrix products: 40.4 us -> 0 us
  starting transfers between devices: 13.5 us -> 0 us
  between operations: 14.1 us -> 0.64 us
  other arithmetic: 5.48 us -> 0 us
    psum x1 -> x0, waiting for transfers between devices: 131 us -> none  [per_device(): block_totals = lax.psum(jnp.stack(term_list), ('row', 'col'))]
    pallas_call x0 -> x1, Pallas kernels: none -> 129 us  [per_device(): pl.pallas_call(functools.partial(kernel, sizes), out_shape=(jax.ShapeDtyp...]
    reduce_scatter x3 -> x0, waiting for transfers between devices: 92.8 us -> none  [per_device(): lax.psum_scatter(partial_value, 'col', scatter_dimension=0, tiled=True)]
    dot_general x20 -> x0, matrix products: 40.4 us -> none  [the longest x3 22.1 us: per_device(): jnp.einsum('rc,mcw->rmw', trailing_inverse, gathered, precision=lax.Preci...]
    all_to_all x3 -> x0, blocking collectives: 34.1 us -> none  [the longest x2 19.6 us: per_device(): lax.all_to_all(lax.all_to_all(sender, 'col', split_axis=1, concat_axis=1,...]
    all_gather x3 -> x0, blocking collectives: 27.5 us -> none  [per_device(): lax.all_gather(factor_cols[first_node:first_node + group_size], 'row', ax...]
    all_to_all x3 -> x0, waiting for transfers between devices: 25.2 us -> none  [the longest x2 18.2 us: per_device(): lax.all_to_all(sender, 'col', split_axis=1, concat_axis=1, tiled=True)]
    all_to_all x3 -> x0, starting transfers between devices: 12.9 us -> none  [the longest x2 9.45 us: per_device(): lax.all_to_all(sender, 'col', split_axis=1, concat_axis=1, tiled=True)]
  transfers between devices with their start and end apart: 7 -> 0, of which waited for: 6 -> 0; matrix products, arithmetic and copies ran while one was open for 6% -> 0% of each run, Pallas kernels for 0% -> 0%
where the time goes in v1:
time: 137 us; the launch traced here: 136 us
  Pallas kernels  129 us (94%)
  local copies, waits for them, and re-layouts  6.04 us (4%)
    pallas_call x1, Pallas kernels, per_device(): pl.pallas_call(functools.partial(kernel, sizes), out_shape=(jax.ShapeDtyp...  129 us
    unnamed x3, local copies, waits for them, and re-layouts  6.04 us

profile of v1, /device:TPU:0, one launch (start us, length us, event | category | flops | bytes accessed | tf_op | source)
XLA Modules:
  0.0 136.0 jit_solution(8363226135759938360)
XLA Ops:
  0.6 129.3 %shard_map.67 = (f32[3,192,256]{2,1,0:T(8,128)}, f32[3,256,256]{2,1,0:T(8,128)}, f32[3,256,256]{2,1,0:T(8,128)}) custom-call(f32[1536,768]{1,0:T(8,128)} %t_hbm.1, f32[3,192,256]{2,1,0:T(8,128)} %f_ref.1, f32[3,256,256]{2,1,0:T(8,128)} %b_ref.1, f32[3,256,256]{2,1,0:T(8,128)} %d_ref.1), custom_call_target="tpu_custom_call" | custom-call | tf_op jit(solution)/shard_map/pallas_call | solution.py:395
  130.0 1.9 %copy.10 = f32[3,192,256]{2,1,0:T(8,128)} copy(f32[3,192,256]{2,1,0:T(8,128)} %get-tuple-element.6) | data formatting | bytes 1179648
  131.9 2.1 %copy.11 = f32[3,256,256]{2,1,0:T(8,128)} copy(f32[3,256,256]{2,1,0:T(8,128)} %get-tuple-element.7) | data formatting | bytes 1572864
  134.0 2.1 %copy.12 = f32[3,256,256]{2,1,0:T(8,128)} copy(f32[3,256,256]{2,1,0:T(8,128)} %get-tuple-element.8) | data formatting | bytes 1572864

commit v2 on v1

--- a/solution.py
+++ b/solution.py
@@ -11,20 +11,22 @@
 CORES = 2
 
 
-def exact_dot(left, right, left_dim=1):
-    return lax.dot_general(
-        left,
-        right,
-        (((left_dim,), (0,)), ((), ())),
-        precision=lax.Precision.HIGHEST,
-        preferred_element_type=jnp.float32,
-    )
-
-
 def split(value):
     high = value.astype(jnp.bfloat16)
     low = (value - high.astype(jnp.float32)).astype(jnp.bfloat16)
     return high, low
+
+
+def exact_dot(left, right, left_dim=1):
+    left_high, left_low = split(left)
+    right_high, right_low = split(right)
+    value = None
+    for one, two in ((left_high, right_high), (left_low, right_high), (left_high, right_low)):
+        term = lax.dot_general(
+            one, two, (((left_dim,), (0,)), ((), ())), preferred_element_type=jnp.float32
+        )
+        value = term if value is None else value + term
+    return value
 
 
 def pair_order(node_count):
@@ -269,10 +271,24 @@
 
         def step4(self):
             self.receive()
+            self.pass_on = []
             group = (r // self.splits) * self.splits
-            for dr in range(1, self.splits):
-                ref = self.out.at[self.share_of(r)]
-                self.send(ref, ref, group + (r - group + dr) % self.splits, c)
+            ref = self.out.at[self.share_of(r)]
+            near = group + (r - group) // CORES * CORES + 1 - core
+            for step in range(CORES, self.splits, CORES):
+                ahead = group + (r - group + step) % self.splits
+                self.send(ref, ref, ahead, c)
+                behind = group + (r - group - step + self.splits) % self.splits
+                self.pass_on.append((self.copies.pop(), behind))
+            if self.splits > 1:
+                self.send(ref, ref, near, c)
+
+        def step5(self):
+            for copy, row in self.pass_on:
+                copy.wait_recv()
+                ref = self.out.at[self.share_of(row)]
+                self.send(ref, ref, sibling, c)
+            self.receive()
 
     per_total = 2 * (row_count - 1) + 2 * (col_count - 1)
     many, last = Total(stages[0], base), Total(stages[1], base + per_total)
@@ -320,7 +336,7 @@
     last.step2()
     many.step4()
     last.step3()
-    many.receive()
+    many.step5()
 
     for node in order:
         for later in range(node + 1, nodes):
@@ -342,7 +358,7 @@
             value -= exact_dot(b_ref[pair], cross_ref[pair], 0)
         diag_ref[node] = value
     last.step4()
-    last.receive()
+    last.step5()
     diag_ref[0] = diag_ref[0] - last.out[...]
 
     for copy in started:

time: 137 us -> 131 us (0.956)
  Pallas kernels: 129 us -> 124 us
    pallas_call x1, Pallas kernels: 129 us -> 124 us  [per_device(): pl.pallas_call(functools.partial(kernel, sizes), out_shape=(jax.ShapeDtyp...]
where the time goes in v2:
time: 131 us
  Pallas kernels  124 us (95%)
  local copies, waits for them, and re-layouts  6.04 us (5%)
    pallas_call x1, Pallas kernels, per_device(): pl.pallas_call(functools.partial(kernel, sizes), out_shape=(jax.ShapeDtyp...  124 us
    unnamed x3, local copies, waits for them, and re-layouts  6.04 us

profile of v2, /device:TPU:0, one launch (start us, length us, event | category | flops | bytes accessed | tf_op | source)
XLA Modules:
  0.0 130.7 jit_solution(13763902513898718086)
XLA Ops:
  0.6 124.0 %shard_map.67 = (f32[3,192,256]{2,1,0:T(8,128)}, f32[3,256,256]{2,1,0:T(8,128)}, f32[3,256,256]{2,1,0:T(8,128)}) custom-call(f32[1536,768]{1,0:T(8,128)} %t_hbm.1, f32[3,192,256]{2,1,0:T(8,128)} %f_ref.1, f32[3,256,256]{2,1,0:T(8,128)} %b_ref.1, f32[3,256,256]{2,1,0:T(8,128)} %d_ref.1), custom_call_target="tpu_custom_call" | custom-call | tf_op jit(solution)/shard_map/pallas_call | solution.py:411
  124.6 1.9 %copy.10 = f32[3,192,256]{2,1,0:T(8,128)} copy(f32[3,192,256]{2,1,0:T(8,128)} %get-tuple-element.6) | data formatting | bytes 1179648
  126.5 2.1 %copy.11 = f32[3,256,256]{2,1,0:T(8,128)} copy(f32[3,256,256]{2,1,0:T(8,128)} %get-tuple-element.7) | data formatting | bytes 1572864
  128.6 2.1 %copy.12 = f32[3,256,256]{2,1,0:T(8,128)} copy(f32[3,256,256]{2,1,0:T(8,128)} %get-tuple-element.8) | data formatting | bytes 1572864
